TPU v7x, 128 devices: a whole 4x4x4 slice. The times are simulated.
128 devices in a mesh: blk: 32 (over x_lo, z, y), rad: 4 (over x_hi, core).
Axes of the slice: x: 4 (x_hi: 2, x_lo: 2; x = x_hi * 2 + x_lo), y: 4, z: 4, core: 2. Of those that a mesh axis runs over, the one named last changes fastest.
Arguments:
- right_side: float32 [512, 2, 32, 4096], P(None, None, 'rad', 'blk'), may hold values from -6 to 6
- coefficient: float32 [512, 2, 32, 4096], P(None, None, 'rad', 'blk'), may hold values from 0.5 to 2
- geometry: float32 [3, 2, 32, 4096], P(None, None, 'rad', 'blk'), may hold values from 0.002 to 0.02
- interp: float32 [4, 64, 64], replicated, may hold values from -0.3 to 1.35
- face_map: int32 [32, 4096], P('rad', 'blk'), may hold values from 0 to 3
- offset: int32 [1], replicated, may hold values from 0 to 262143
Outputs:
- solution_field: float32 [512, 2, 32, 4096], P(None, None, 'rad', 'blk')
- residual: float32 [512, 2, 32, 4096], P(None, None, 'rad', 'blk')
All inputs are finite; a program needn't handle non-finite values.
Results may differ from a plain program's by a relative error of at most 0.00011.
Values sent between devices are 32-bit elements; how exact they have to be, the bound alone decides.
A program may use at most 128 MiB of HBM per device.

v0:
```python
import jax
import jax.numpy as jnp
from jax import lax
from jax.sharding import PartitionSpec as P

ITERS = 3


PENALTY = 1.0
HIGHEST = lax.Precision.HIGHEST


def from_behind(array, axis, by):
    size = lax.axis_size(axis)
    return lax.ppermute(array, axis, [(i, (i + by) % size) for i in range(size)])


def extended(cells, sides, width, closed):
    for axis, dim in sides:
        count = lax.axis_size(axis)
        ends = count if closed else count - 1
        head = lax.slice_in_dim(cells, 0, width, axis=dim)
        tail = lax.slice_in_dim(cells, cells.shape[dim] - width, cells.shape[dim], axis=dim)
        cells = jnp.concatenate(
            [
                lax.ppermute(tail, axis, [(i, (i + 1) % count) for i in range(ends)]),
                cells,
                lax.ppermute(head, axis, [((i + 1) % count, i) for i in range(ends)]),
            ],
            axis=dim,
        )
    return cells


def spectral_derivative():
    counter = jnp.arange(8)
    points = -jnp.cos(jnp.pi * counter.astype(jnp.float32) / 7.0)
    endpoint = jnp.logical_or(counter == 0, counter == 7)
    weights = jnp.where(endpoint, 2.0, 1.0).astype(jnp.float32)
    parity = 1.0 - 2.0 * ((counter[:, None] + counter[None, :]) % 2).astype(jnp.float32)
    diagonal_mask = counter[:, None] == counter[None, :]
    spacing = jnp.where(diagonal_mask, 1.0, points[:, None] - points[None, :])
    off_terms = jnp.where(
        diagonal_mask, 0.0, weights[:, None] / weights[None, :] * parity / spacing
    )
    return off_terms - jnp.diag(jnp.sum(off_terms, axis=1))


def element_part(nodal, coefficient, geometry, derivative):
    flat_nodes = nodal.reshape(8, 8, 8, -1)
    factors = geometry.reshape(3, -1)
    result = coefficient.reshape(8, 8, 8, -1) * flat_nodes
    grad_one = jnp.einsum("ai,ijkx->ajkx", derivative, flat_nodes, precision=HIGHEST)
    result = result + jnp.einsum(
        "ai,ajkx->ijkx", derivative, grad_one * factors[0], precision=HIGHEST
    )
    grad_two = jnp.einsum("bj,ijkx->ibkx", derivative, flat_nodes, precision=HIGHEST)
    result = result + jnp.einsum(
        "bj,ibkx->ijkx", derivative, grad_two * factors[1], precision=HIGHEST
    )
    grad_three = jnp.einsum("ck,ijkx->ijcx", derivative, flat_nodes, precision=HIGHEST)
    result = result + jnp.einsum(
        "ck,ijcx->ijkx", derivative, grad_three * factors[2], precision=HIGHEST
    )
    return result.reshape(nodal.shape)


def block_pick(interp, face_map):
    return (face_map[None] == jnp.arange(interp.shape[0])[:, None, None]).astype(jnp.float32)


def interface_jump(rotor_side, stator_side, interp, face_map):
    mapped = jnp.einsum("mpq,qrc->mprc", interp, rotor_side, precision=HIGHEST)
    picked = block_pick(interp, face_map)
    return jnp.sum(picked[:, None] * mapped, axis=0) - stator_side


def interface_back(face_jump, interp, face_map):
    mapped = jnp.einsum("mqp,qrc->mprc", interp, face_jump, precision=HIGHEST)
    picked = block_pick(interp, face_map)
    return jnp.sum(picked[:, None] * mapped, axis=0)


def squares_sum(residual):
    return lax.psum(jnp.sum(residual * residual), ("blk", "rad"))


def on_device(right_side, coefficient, geometry, interp, face_map, offset):
    derivative = spectral_derivative()
    cycle_size = lax.axis_size("blk")
    layers = right_side.shape[1]
    radial = right_side.shape[2]
    cycle_cells = right_side.shape[3]
    bit_count = max((cycle_size - 1).bit_length(), 1)
    rotation = offset[0] % (cycle_cells * cycle_size)
    cycle_hops = rotation // cycle_cells
    remain = rotation - cycle_hops * cycle_cells
    lower_open = (lax.axis_index("rad") > 0).astype(jnp.float32)
    upper_open = (lax.axis_index("rad") < lax.axis_size("rad") - 1).astype(jnp.float32)
    solution_field = jnp.zeros_like(right_side)
    residual = right_side
    direction = right_side
    norm_now = squares_sum(residual)
    for iteration in range(ITERS):
        nodal = direction.reshape(8, 8, 8, layers, radial, cycle_cells)
        result = element_part(nodal, coefficient, geometry, derivative)
        top_face = nodal[:, 7]
        bottom_face = nodal[:, 0]
        radial_rims = jnp.stack([bottom_face[:, :, :, 0], top_face[:, :, :, radial - 1]]).reshape(
            2, -1
        )
        radial_padded = extended(radial_rims, (("rad", 0),), 1, False)
        below_top = radial_padded[0].reshape(8, 8, layers, cycle_cells)
        above_bottom = radial_padded[3].reshape(8, 8, layers, cycle_cells)
        inner_jump = top_face[:, :, :, :-1] - bottom_face[:, :, :, 1:]
        low_jump = below_top - bottom_face[:, :, :, 0]
        high_jump = top_face[:, :, :, radial - 1] - above_bottom
        upper_terms = jnp.concatenate([inner_jump, (upper_open * high_jump)[:, :, :, None]], axis=3)
        lower_terms = jnp.concatenate([(lower_open * low_jump)[:, :, :, None], inner_jump], axis=3)
        result = result.at[:, 7].add(PENALTY * upper_terms)
        result = result.at[:, 0].add(-PENALTY * lower_terms)
        right_face = nodal[:, :, 7]
        left_face = nodal[:, :, 0]
        cycle_rims = jnp.stack([left_face[..., 0], right_face[..., cycle_cells - 1]]).reshape(2, -1)
        cycle_padded = extended(cycle_rims, (("blk", 0),), 1, True)
        prior_right = cycle_padded[0].reshape(8, 8, layers, radial)
        next_left = cycle_padded[3].reshape(8, 8, layers, radial)
        left_ahead = jnp.concatenate([left_face[..., 1:], next_left[..., None]], axis=4)
        circ_jump = right_face - left_ahead
        first_jump = prior_right - left_face[..., 0]
        circ_back = jnp.concatenate([first_jump[..., None], circ_jump[..., :-1]], axis=4)
        result = result.at[:, :, 7].add(PENALTY * circ_jump)
        result = result.at[:, :, 0].add(-PENALTY * circ_back)
        rotor_face = nodal[7, :, :, 0].reshape(64, radial, cycle_cells)
        stator_face = nodal[0, :, :, 1].reshape(64, radial, cycle_cells)
        sectioned_current = rotor_face
        for sectioned_bit_index in range(bit_count):
            sectioned_shifted = from_behind(sectioned_current, "blk", 1 << sectioned_bit_index)
            sectioned_current = jnp.where(
                (cycle_hops >> sectioned_bit_index) % 2 == 1, sectioned_shifted, sectioned_current
            )
        earlier = from_behind(sectioned_current, "blk", 1)
        sectioned_doubled = jnp.concatenate([earlier, sectioned_current], axis=2)
        turned = lax.dynamic_slice_in_dim(sectioned_doubled, cycle_cells - remain, cycle_cells, 2)
        face_jump = interface_jump(turned, stator_face, interp, face_map)
        current = interface_back(face_jump, interp, face_map)
        for bit_index in range(bit_count):
            shifted = from_behind(current, "blk", -(1 << bit_index))
            current = jnp.where((cycle_hops >> bit_index) % 2 == 1, shifted, current)
        later = from_behind(current, "blk", -1)
        doubled = jnp.concatenate([current, later], axis=2)
        returned = lax.dynamic_slice_in_dim(doubled, remain, cycle_cells, 2)
        result = result.at[7, :, :, 0].add(PENALTY * returned.reshape(8, 8, radial, cycle_cells))
        result = result.at[0, :, :, 1].add(-PENALTY * face_jump.reshape(8, 8, radial, cycle_cells))
        image = result.reshape(direction.shape)
        alpha = norm_now / lax.psum(jnp.sum(direction * image), ("blk", "rad"))
        solution_field = solution_field + alpha * direction
        residual = residual - alpha * image
        norm_next = squares_sum(residual)
        direction = residual + norm_next / norm_now * direction
        norm_now = norm_next
    return (solution_field, residual)


def solution(mesh):
    placed = (
        P(None, None, "rad", "blk"),
        P(None, None, "rad", "blk"),
        P(None, None, "rad", "blk"),
        P(),
        P("rad", "blk"),
        P(),
    )
    return jax.shard_map(
        on_device,
        mesh=mesh,
        in_specs=placed,
        out_specs=(P(None, None, "rad", "blk"), P(None, None, "rad", "blk")),
        check_vma=False,
    )
```

profile of v0, /device:TPU:1, one launch (start us, length us, event | category | flops | bytes accessed | tf_op | source)
XLA Modules:
  0.0 958.1 jit_solution(13496725796778838262)
XLA Ops:
  69.9 13.5 %bitcast_add_fusion.4 = f32[8,8,8,2048]{3,0,2,1:T(8,128)} fusion(f32[8,8,2048,8]{2,3,1,0:T(8,128)S(1)} %fusion.14, f32[8,8,2048,8]{2,3,1,0:T(8,128)S(1)} %fusion.16, f32[8,8,8,2048]{3,2,1,0:T(8,128)S(1)} %copy-done.4, f32[8,8,8,2048]{3,2,1,0:T(8,128)S(1)} %copy-done.8, f32[8,8,8,2048]{3,0,2,1:T(8,128)S(1)} %fusion.40, f32[2048]{0:T(1024)S(1)} %get-tuple-element.260, ...), kind=kOutput, calls=%fused_computation.24 | convolution fusion | flops 105907712 | bytes 25174112 | tf_op jit(solution)/shard_map/ai,ajkx->ijkx/dot_general | solution.py:54
  154.6 14.3 %scatter-add.64 = f32[8,8,8,2,8,128]{5,2,4,3,0,1:T(8,128)} dynamic-update-slice(f32[8,8,8,2,8,128]{5,2,4,3,0,1:T(8,128)} %fusion.75, f32[8,8,1,2,8,128]{5,2,4,3,0,1:T(1,128)S(1)} %slice_add_fusion.8, s32[]{:T(128)} %constant.530.clone.1, s32[]{:T(128)} %constant.530.clone.1, s32[]{:T(128)} %constant.531.clone.1, s32[]{:T(128)} %constant.530.clone.1, s32[]{:T(128)} %constant.530.clone.1, ...) | dynamic-update-slice | bytes 1048580 | tf_op jit(solution)/shard_map/scatter-add | solution.py:132
  173.8 14.3 %scatter-add.65 = f32[8,8,8,2,8,128]{5,2,4,3,0,1:T(8,128)} dynamic-update-slice(f32[8,8,8,2,8,128]{5,2,4,3,0,1:T(8,128)} %scatter-add.64, f32[8,8,1,2,8,128]{5,2,4,3,0,1:T(1,128)S(1)} %slice_add_fusion.7, s32[]{:T(128)} %constant.530.clone.1, s32[]{:T(128)} %constant.530.clone.1, s32[]{:T(128)} %constant.530.clone.1, s32[]{:T(128)} %constant.530.clone.1, s32[]{:T(128)} %constant.530.clone.1, ...) | dynamic-update-slice | bytes 1048580 | tf_op jit(solution)/shard_map/scatter-add | solution.py:133
  198.4 67.4 %all-reduce = (f32[]{:T(128)}, f32[]{:T(128)}) all-reduce(f32[]{:T(128)} %get-tuple-element.219, f32[]{:T(128)} %get-tuple-element.218), channel_id=1, replica_groups=mesh['blk'=32,'rad'=4] {'blk','rad'}, use_global_device_ids=true, to_apply=%region_1.2 | all-reduce | flops 2 | bytes 16 | tf_op jit(solution)/shard_map/psum | solution.py:85
  272.1 62.5 %psum.44 = f32[]{:T(128)} all-reduce(f32[]{:T(128)} %multiply_reduce_fusion.1), channel_id=1, replica_groups=mesh['blk'=32,'rad'=4] {'blk','rad'}, use_global_device_ids=true, to_apply=%region_9.10 | all-reduce | flops 1 | bytes 8 | tf_op jit(solution)/shard_map/psum | solution.py:85
  384.4 7.8 fusion.20
  409.3 13.7 %bitcast_add_fusion.2 = f32[8,8,8,2048]{3,0,2,1:T(8,128)} fusion(f32[8,8,2048,8]{2,3,1,0:T(8,128)S(1)} %fusion.8, f32[8,8,2048,8]{2,3,1,0:T(8,128)S(1)} %fusion.10, f32[8,8,8,2048]{3,2,1,0:T(8,128)S(1)} %copy-done.5, f32[8,8,8,2048]{3,2,1,0:T(8,128)S(1)} %copy-done.9, f32[8,8,8,2048]{3,0,2,1:T(8,128)S(1)} %fusion.38, f32[2048]{0:T(1024)S(1)} %get-tuple-element.260, ...), kind=kOutput, calls=%fused_computation.14 | convolution fusion | flops 105907712 | bytes 25174112 | tf_op jit(solution)/shard_map/ai,ajkx->ijkx/dot_general | solution.py:54
  447.2 6.8 copy.663
  489.1 14.3 %scatter-add.74 = f32[8,8,8,2,8,128]{5,2,4,3,0,1:T(8,128)} dynamic-update-slice(f32[8,8,8,2,8,128]{5,2,4,3,0,1:T(8,128)} %fusion.72, f32[8,8,1,2,8,128]{5,2,4,3,0,1:T(1,128)S(1)} %bitcast.427, s32[]{:T(128)} %constant.530.clone.1, s32[]{:T(128)} %constant.530.clone.1, s32[]{:T(128)} %constant.531.clone.1, s32[]{:T(128)} %constant.530.clone.1, s32[]{:T(128)} %constant.530.clone.1, s32[]{:T(128)} %constant.530.clone.1) | dynamic-update-slice | bytes 1048580 | tf_op jit(solution)/shard_map/scatter-add | solution.py:132
  504.4 7.6 collective-permute-start.31
  515.7 14.3 %scatter-add.75 = f32[8,8,8,2,8,128]{5,2,4,3,0,1:T(8,128)} dynamic-update-slice(f32[8,8,8,2,8,128]{5,2,4,3,0,1:T(8,128)} %scatter-add.74, f32[8,8,1,2,8,128]{5,2,4,3,0,1:T(1,128)S(1)} %slice_add_fusion.4, s32[]{:T(128)} %constant.530.clone.1, s32[]{:T(128)} %constant.530.clone.1, s32[]{:T(128)} %constant.530.clone.1, s32[]{:T(128)} %constant.530.clone.1, s32[]{:T(128)} %constant.530.clone.1, ...) | dynamic-update-slice | bytes 1048580 | tf_op jit(solution)/shard_map/scatter-add | solution.py:133
  541.8 63.5 %psum.45 = f32[]{:T(128)} all-reduce(f32[]{:T(128)} %fusion.6), channel_id=1, replica_groups=mesh['blk'=32,'rad'=4] {'blk','rad'}, use_global_device_ids=true, to_apply=%region_13.14 | all-reduce | flops 1 | bytes 8 | tf_op jit(solution)/shard_map/psum | solution.py:156
  606.6 8.3 multiply_reduce_fusion
  614.9 63.5 %psum.46 = f32[]{:T(128)} all-reduce(f32[]{:T(128)} %get-tuple-element.222), channel_id=1, replica_groups=mesh['blk'=32,'rad'=4] {'blk','rad'}, use_global_device_ids=true, to_apply=%region_15.16 | all-reduce | flops 1 | bytes 8 | tf_op jit(solution)/shard_map/psum | solution.py:85
  693.9 9.5 fusion.138
  716.7 7.8 fusion.18
  742.7 13.5 %bitcast_add_fusion = f32[8,8,8,2048]{3,0,2,1:T(8,128)} fusion(f32[8,8,2048,8]{2,3,1,0:T(8,128)S(1)} %fusion.2, f32[8,8,2048,8]{2,3,1,0:T(8,128)S(1)} %fusion.4, f32[8,8,8,2048]{3,2,1,0:T(8,128)S(1)} %copy-done.6, f32[8,8,8,2048]{3,2,1,0:T(8,128)S(1)} %copy-done.10, f32[8,8,8,2048]{3,0,2,1:T(8,128)S(1)} %fusion.36, f32[2048]{0:T(1024)S(1)} %get-tuple-element.260, ...), kind=kOutput, calls=%fused_computation.4 | convolution fusion | flops 105907712 | bytes 25174112 | tf_op jit(solution)/shard_map/ai,ajkx->ijkx/dot_general | solution.py:54
  775.8 6.8 copy.704
  783.2 12.1 %collective-permute-start.33 = (f32[1,16384]{1,0:T(1,128)}, f32[1,16384]{1,0:T(1,128)}, u32[]{:S(2)}, u32[]{:S(2)}) collective-permute-start(f32[1,16384]{1,0:T(1,128)} %bitcast.97), channel_id=1, source_target_pairs={{0,1},{1,2},{2,3},{4,5},{5,6},{6,7},{8,9},{9,10},{10,11},{12,13},{... | collective-permute-start | bytes 196616 | tf_op jit(solution)/shard_map/ppermute | solution.py:26
  829.9 14.3 %scatter-add.84 = f32[8,8,8,2,8,128]{5,2,4,3,0,1:T(8,128)} dynamic-update-slice(f32[8,8,8,2,8,128]{5,2,4,3,0,1:T(8,128)} %fusion.70, f32[8,8,1,2,8,128]{5,2,4,3,0,1:T(1,128)S(1)} %slice_add_fusion.1, s32[]{:T(128)} %constant.530.clone.1, s32[]{:T(128)} %constant.530.clone.1, s32[]{:T(128)} %constant.531.clone.1, s32[]{:T(128)} %constant.530.clone.1, s32[]{:T(128)} %constant.530.clone.1, ...) | dynamic-update-slice | bytes 1048580 | tf_op jit(solution)/shard_map/scatter-add | solution.py:132
  845.2 7.2 collective-permute-start.47
  855.3 14.3 %scatter-add.85 = f32[8,8,8,2,8,128]{5,2,4,3,0,1:T(8,128)} dynamic-update-slice(f32[8,8,8,2,8,128]{5,2,4,3,0,1:T(8,128)} %scatter-add.84, f32[8,8,1,2,8,128]{5,2,4,3,0,1:T(1,128)S(1)} %slice_add_fusion, s32[]{:T(128)} %constant.530.clone.1, s32[]{:T(128)} %constant.530.clone.1, s32[]{:T(128)} %constant.530.clone.1, s32[]{:T(128)} %constant.530.clone.1, s32[]{:T(128)} %constant.530.clone.1, ...) | dynamic-update-slice | bytes 1048580 | tf_op jit(solution)/shard_map/scatter-add | solution.py:133
  881.4 64.1 %psum.47 = f32[]{:T(128)} all-reduce(f32[]{:T(128)} %fusion), channel_id=1, replica_groups=mesh['blk'=32,'rad'=4] {'blk','rad'}, use_global_device_ids=true, to_apply=%region_19.20 | all-reduce | flops 1 | bytes 8 | tf_op jit(solution)/shard_map/psum | solution.py:156
  946.9 7.7 multiply_add_fusion
  (362 shorter events, 419.8 us)
Async XLA Ops:
  2.9 119.0 %collective-permute-start.1 = (f32[1,16384]{1,0:T(1,128)}, f32[1,16384]{1,0:T(1,128)}, u32[]{:S(2)}, u32[]{:S(2)}) collective-permute-start(f32[1,16384]{1,0:T(1,128)} %bitcast.20), channel_id=1, source_target_pairs={{0,1},{1,2},{2,3},{4,5},{5,6},{6,7},{8,9},{9,10},{10,11},{12,13},{... | collective-permute-start | bytes 196616 | tf_op jit(solution)/shard_map/ppermute | solution.py:26
  11.5 76.7 %collective-permute-start.3 = (f32[1,1024]{1,0:T(1,128)S(1)}, f32[1,1024]{1,0:T(1,128)S(1)}, u32[]{:S(2)}, u32[]{:S(2)}) collective-permute-start(f32[1,1024]{1,0:T(1,128)S(1)} %slice.900), channel_id=1, source_target_pairs={{0,4},{4,8},{8,12},{12,16},{16,20},{20,24},{24,28},{28,32},{32,36}... | collective-permute-start | bytes 12296 | tf_op jit(solution)/shard_map/ppermute | solution.py:26
  14.0 23.0 %collective-permute-start.4 = (f32[64,8,128]{2,0,1:T(8,128)S(1)}, f32[64,8,128]{2,0,1:T(8,128)}, u32[]{:S(2)}, u32[]{:S(2)}) collective-permute-start(f32[64,8,128]{2,0,1:T(8,128)S(1)} %bitcast.441), channel_id=1, source_target_pairs={{0,4},{4,8},{8,12},{12,16},{16,20},{20,24},{24,28},{28,32},{32,36}... | collective-permute-start | bytes 786440 | tf_op jit(solution)/shard_map/ppermute | solution.py:15
  69.7 14.8 %collective-permute-start.8 = (f32[64,8,128]{2,0,1:T(8,128)S(1)}, f32[64,8,128]{2,0,1:T(8,128)S(1)}, u32[]{:S(2)}, u32[]{:S(2)}) collective-permute-start(f32[64,8,128]{2,0,1:T(8,128)S(1)} %broadcast_select_fusion.23), channel_id=1, source_target_pairs={{0,64},{4,68},{8,72},{12,76},{16,80},{20,84},{24,88},{28,92},{32,9... | collective-permute-start | bytes 786440 | tf_op jit(solution)/shard_map/ppermute | solution.py:15
  98.6 21.9 %collective-permute-start.10 = (f32[64,8,128]{2,0,1:T(8,128)}, f32[64,8,128]{2,0,1:T(8,128)}, u32[]{:S(2)}, u32[]{:S(2)}) collective-permute-start(f32[64,8,128]{2,0,1:T(8,128)} %fusion.67), channel_id=1, source_target_pairs={{0,124},{4,0},{8,4},{12,8},{16,12},{20,16},{24,20},{28,24},{32,28}... | collective-permute-start | bytes 786440 | tf_op jit(solution)/shard_map/ppermute | solution.py:15
  103.3 14.8 %collective-permute-start.2 = (f32[1,1024]{1,0:T(1,128)S(1)}, f32[1,1024]{1,0:T(1,128)S(1)}, u32[]{:S(2)}, u32[]{:S(2)}) collective-permute-start(f32[1,1024]{1,0:T(1,128)S(1)} %slice.897), channel_id=1, source_target_pairs={{4,0},{8,4},{12,8},{16,12},{20,16},{24,20},{28,24},{32,28},{36,32}... | collective-permute-start | bytes 12296 | tf_op jit(solution)/shard_map/ppermute | solution.py:28
  149.4 19.4 %collective-permute-start.14 = (f32[64,8,128]{2,0,1:T(8,128)S(1)}, f32[64,8,128]{2,0,1:T(8,128)}, u32[]{:S(2)}, u32[]{:S(2)}) collective-permute-start(f32[64,8,128]{2,0,1:T(8,128)S(1)} %broadcast_select_fusion.22), channel_id=1, source_target_pairs={{0,64},{4,68},{8,72},{12,76},{16,80},{20,84},{24,88},{28,92},{32,9... | collective-permute-start | bytes 786440 | tf_op jit(solution)/shard_map/ppermute | solution.py:15
  169.8 18.2 %collective-permute-start.15 = (f32[64,8,128]{2,0,1:T(8,128)S(1)}, f32[64,8,128]{2,0,1:T(8,128)S(1)}, u32[]{:S(2)}, u32[]{:S(2)}) collective-permute-start(f32[64,8,128]{2,0,1:T(8,128)S(1)} %broadcast_select_fusion.28), channel_id=1, source_target_pairs={{0,124},{4,0},{8,4},{12,8},{16,12},{20,16},{24,20},{28,24},{32,28}... | collective-permute-start | bytes 786440 | tf_op jit(solution)/shard_map/ppermute | solution.py:15
  353.6 105.9 %collective-permute-start.17 = (f32[1,16384]{1,0:T(1,128)}, f32[1,16384]{1,0:T(1,128)}, u32[]{:S(2)}, u32[]{:S(2)}) collective-permute-start(f32[1,16384]{1,0:T(1,128)} %bitcast.61), channel_id=1, source_target_pairs={{0,1},{1,2},{2,3},{4,5},{5,6},{6,7},{8,9},{9,10},{10,11},{12,13},{... | collective-permute-start | bytes 196616 | tf_op jit(solution)/shard_map/ppermute | solution.py:26
  358.6 65.3 %collective-permute-start.19 = (f32[1,1024]{1,0:T(1,128)S(1)}, f32[1,1024]{1,0:T(1,128)S(1)}, u32[]{:S(2)}, u32[]{:S(2)}) collective-permute-start(f32[1,1024]{1,0:T(1,128)S(1)} %slice.925), channel_id=1, source_target_pairs={{0,4},{4,8},{8,12},{12,16},{16,20},{20,24},{24,28},{28,32},{32,36}... | collective-permute-start | bytes 12296 | tf_op jit(solution)/shard_map/ppermute | solution.py:26
  359.7 12.2 %collective-permute-start.20 = (f32[64,8,128]{2,0,1:T(8,128)S(1)}, f32[64,8,128]{2,0,1:T(8,128)S(1)}, u32[]{:S(2)}, u32[]{:S(2)}) collective-permute-start(f32[64,8,128]{2,0,1:T(8,128)S(1)} %bitcast.443), channel_id=1, source_target_pairs={{0,4},{4,8},{8,12},{12,16},{16,20},{20,24},{24,28},{28,32},{32,36}... | collective-permute-start | bytes 786440 | tf_op jit(solution)/shard_map/ppermute | solution.py:15
  372.0 12.2 %collective-permute-start.21 = (f32[64,8,128]{2,0,1:T(8,128)S(1)}, f32[64,8,128]{2,0,1:T(8,128)S(1)}, u32[]{:S(2)}, u32[]{:S(2)}) collective-permute-start(f32[64,8,128]{2,0,1:T(8,128)S(1)} %broadcast_select_fusion.3), channel_id=1, source_target_pairs={{0,8},{4,12},{8,16},{12,20},{16,24},{20,28},{24,32},{28,36},{32,40... | collective-permute-start | bytes 786440 | tf_op jit(solution)/shard_map/ppermute | solution.py:15
  408.8 19.1 %collective-permute-start.25 = (f32[64,8,128]{2,0,1:T(8,128)S(1)}, f32[64,8,128]{2,0,1:T(8,128)}, u32[]{:S(2)}, u32[]{:S(2)}) collective-permute-start(f32[64,8,128]{2,0,1:T(8,128)S(1)} %broadcast_select_fusion.27), channel_id=1, source_target_pairs={{0,4},{4,8},{8,12},{12,16},{16,20},{20,24},{24,28},{28,32},{32,36}... | collective-permute-start | bytes 786440 | tf_op jit(solution)/shard_map/ppermute | solution.py:15
  444.0 13.8 %collective-permute-start.18 = (f32[1,1024]{1,0:T(1,128)S(1)}, f32[1,1024]{1,0:T(1,128)S(1)}, u32[]{:S(2)}, u32[]{:S(2)}) collective-permute-start(f32[1,1024]{1,0:T(1,128)S(1)} %slice.922), channel_id=1, source_target_pairs={{4,0},{8,4},{12,8},{16,12},{20,16},{24,20},{28,24},{32,28},{36,32}... | collective-permute-start | bytes 12296 | tf_op jit(solution)/shard_map/ppermute | solution.py:28
  445.8 21.6 %collective-permute-start.27 = (f32[64,8,128]{2,0,1:T(8,128)}, f32[64,8,128]{2,0,1:T(8,128)}, u32[]{:S(2)}, u32[]{:S(2)}) collective-permute-start(f32[64,8,128]{2,0,1:T(8,128)} %broadcast_select_fusion.2), channel_id=1, source_target_pairs={{0,120},{4,124},{8,0},{12,4},{16,8},{20,12},{24,16},{28,20},{32,24... | collective-permute-start | bytes 786440 | tf_op jit(solution)/shard_map/ppermute | solution.py:15
  488.3 15.1 %collective-permute-start.30 = (f32[64,8,128]{2,0,1:T(8,128)}, f32[64,8,128]{2,0,1:T(8,128)}, u32[]{:S(2)}, u32[]{:S(2)}) collective-permute-start(f32[64,8,128]{2,0,1:T(8,128)} %broadcast_select_fusion.20), channel_id=1, source_target_pairs={{0,64},{4,68},{8,72},{12,76},{16,80},{20,84},{24,88},{28,92},{32,9... | collective-permute-start | bytes 786440 | tf_op jit(solution)/shard_map/ppermute | solution.py:15
  504.4 25.6 %collective-permute-start.31 = (f32[64,8,128]{2,0,1:T(8,128)S(1)}, f32[64,8,128]{2,0,1:T(8,128)S(1)}, u32[]{:S(2)}, u32[]{:S(2)}) collective-permute-start(f32[64,8,128]{2,0,1:T(8,128)S(1)} %broadcast_select_fusion.26), channel_id=1, source_target_pairs={{0,124},{4,0},{8,4},{12,8},{16,12},{20,16},{24,20},{28,24},{32,28}... | collective-permute-start | bytes 786440 | tf_op jit(solution)/shard_map/ppermute | solution.py:15
  704.6 54.3 %collective-permute-start.35 = (f32[1,1024]{1,0:T(1,128)S(1)}, f32[1,1024]{1,0:T(1,128)S(1)}, u32[]{:S(2)}, u32[]{:S(2)}) collective-permute-start(f32[1,1024]{1,0:T(1,128)S(1)} %slice.948), channel_id=1, source_target_pairs={{0,4},{4,8},{8,12},{12,16},{16,20},{20,24},{24,28},{28,32},{32,36}... | collective-permute-start | bytes 12296 | tf_op jit(solution)/shard_map/ppermute | solution.py:26
  742.6 13.6 %collective-permute-start.40 = (f32[64,8,128]{2,0,1:T(8,128)S(1)}, f32[64,8,128]{2,0,1:T(8,128)S(1)}, u32[]{:S(2)}, u32[]{:S(2)}) collective-permute-start(f32[64,8,128]{2,0,1:T(8,128)S(1)} %broadcast_select_fusion.19), channel_id=1, source_target_pairs={{0,64},{4,68},{8,72},{12,76},{16,80},{20,84},{24,88},{28,92},{32,9... | collective-permute-start | bytes 786440 | tf_op jit(solution)/shard_map/ppermute | solution.py:15
  769.8 29.0 %collective-permute-start.42 = (f32[64,8,128]{2,0,1:T(8,128)}, f32[64,8,128]{2,0,1:T(8,128)}, u32[]{:S(2)}, u32[]{:S(2)}) collective-permute-start(f32[64,8,128]{2,0,1:T(8,128)} %fusion.63), channel_id=1, source_target_pairs={{0,124},{4,0},{8,4},{12,8},{16,12},{20,16},{24,20},{28,24},{32,28}... | collective-permute-start | bytes 786440 | tf_op jit(solution)/shard_map/ppermute | solution.py:15
  775.2 21.8 %collective-permute-start.34 = (f32[1,1024]{1,0:T(1,128)S(1)}, f32[1,1024]{1,0:T(1,128)S(1)}, u32[]{:S(2)}, u32[]{:S(2)}) collective-permute-start(f32[1,1024]{1,0:T(1,128)S(1)} %slice.945), channel_id=1, source_target_pairs={{4,0},{8,4},{12,8},{16,12},{20,16},{24,20},{28,24},{32,28},{36,32}... | collective-permute-start | bytes 12296 | tf_op jit(solution)/shard_map/ppermute | solution.py:28
  783.2 17.9 %collective-permute-start.33 = (f32[1,16384]{1,0:T(1,128)}, f32[1,16384]{1,0:T(1,128)}, u32[]{:S(2)}, u32[]{:S(2)}) collective-permute-start(f32[1,16384]{1,0:T(1,128)} %bitcast.97), channel_id=1, source_target_pairs={{0,1},{1,2},{2,3},{4,5},{5,6},{6,7},{8,9},{9,10},{10,11},{12,13},{... | collective-permute-start | bytes 196616 | tf_op jit(solution)/shard_map/ppermute | solution.py:26
  823.5 20.7 %collective-permute-start.46 = (f32[64,8,128]{2,0,1:T(8,128)S(1)}, f32[64,8,128]{2,0,1:T(8,128)}, u32[]{:S(2)}, u32[]{:S(2)}) collective-permute-start(f32[64,8,128]{2,0,1:T(8,128)S(1)} %broadcast_select_fusion.18), channel_id=1, source_target_pairs={{0,64},{4,68},{8,72},{12,76},{16,80},{20,84},{24,88},{28,92},{32,9... | collective-permute-start | bytes 786440 | tf_op jit(solution)/shard_map/ppermute | solution.py:15
  845.2 24.4 %collective-permute-start.47 = (f32[64,8,128]{2,0,1:T(8,128)S(1)}, f32[64,8,128]{2,0,1:T(8,128)S(1)}, u32[]{:S(2)}, u32[]{:S(2)}) collective-permute-start(f32[64,8,128]{2,0,1:T(8,128)S(1)} %broadcast_select_fusion.24), channel_id=1, source_target_pairs={{0,124},{4,0},{8,4},{12,8},{16,12},{20,16},{24,20},{28,24},{32,28}... | collective-permute-start | bytes 786440 | tf_op jit(solution)/shard_map/ppermute | solution.py:15
  (62 other events, 951.7 us)
where the time goes:
time: 970 us; the launch traced here: 958 us
  blocking collectives  321 us (33%)
  local copies, waits for them, and re-layouts  212 us (22%)
  matrix products  147 us (15%)
  other arithmetic  122 us (13%)
  starting transfers between devices  85.1 us (9%)
  waiting for transfers between devices  62 us (6%)
    psum x3, blocking collectives, squares_sum(): return lax.psum(jnp.sum(residual * residual), ('blk', 'rad'))  193 us
    psum x2, blocking collectives, on_device(): alpha = norm_now / lax.psum(jnp.sum(direction * image), ('blk', 'rad'))  128 us
    ppermute x36, waiting for transfers between devices, from_behind(): lax.ppermute(array, axis, [(i, (i + by) % size) for i in range(size)])  62 us
    ppermute x36, starting transfers between devices, from_behind(): lax.ppermute(array, axis, [(i, (i + by) % size) for i in range(size)])  47.4 us
    scatter-add x3, local copies, waits for them, and re-layouts, on_device(): result = result.at[:, :, 0].add(-PENALTY * circ_back)  42.8 us
    scatter-add x3, local copies, waits for them, and re-layouts, on_device(): result = result.at[:, :, 7].add(PENALTY * circ_jump)  42.8 us
    dot_general x3, matrix products, element_part(): jnp.einsum('ai,ajkx->ijkx', derivative, grad_one * factors[0], precision=...  40.7 us
    ppermute x6, starting transfers between devices, extended(): lax.ppermute(tail, axis, [(i, (i + 1) % count) for i in range(ends)])  24.4 us
  transfers between devices with their start and end apart: 48, of which 20 were waited for; matrix products, arithmetic and copies ran while one was open for 38% of the time, Pallas kernels for 0%

commit v1 on v0

v1 whole, which is shorter than its diff:
```python
import functools

import jax
import jax.numpy as jnp
import numpy as np
from jax import lax
from jax.experimental import pallas as pl
from jax.experimental.pallas import tpu as pltpu
from jax.sharding import PartitionSpec as P

ITERS = 3
MESH = pl.DeviceIdType.MESH
F32 = jnp.float32
BF16 = jnp.bfloat16


def stiffness_halves():
    n = np.arange(8)
    x = -np.cos(np.pi * n / 7.0)
    c = np.where((n == 0) | (n == 7), 2.0, 1.0)
    sign = 1.0 - 2.0 * ((n[:, None] + n[None, :]) % 2)
    gap = x[:, None] - x[None, :] + np.eye(8)
    d = (c[:, None] / c[None, :]) * sign / gap * (1.0 - np.eye(8))
    d = d - np.diag(d.sum(axis=1))
    k = d.T @ d
    mirror = k[:4, ::-1][:, :4]
    return 0.5 * (k[:4, :4] + mirror), 0.5 * (k[:4, :4] - mirror)


EVEN, ODD = stiffness_halves()


def line_apply(v):
    sums = [v[m] + v[7 - m] for m in range(4)]
    diffs = [v[m] - v[7 - m] for m in range(4)]
    out = [None] * 8
    for m in range(4):
        e = sums[0] * float(EVEN[m, 0])
        o = diffs[0] * float(ODD[m, 0])
        for n in range(1, 4):
            e = e + sums[n] * float(EVEN[m, n])
            o = o + diffs[n] * float(ODD[m, n])
        out[m] = e + o
        out[7 - m] = e - o
    return out


def split_rows(a):
    high = a.astype(BF16)
    low = (a - high.astype(F32)).astype(BF16)
    return jnp.concatenate([high, low, high, low], axis=0)


def split_columns(p):
    both = jnp.concatenate([p, p], axis=1)
    high = both.astype(BF16)
    low = (both - high.astype(F32)).astype(BF16)
    return jnp.concatenate([high, low], axis=1)


def choose(blocks, which):
    which = jnp.broadcast_to(which, (64, 128))
    out = blocks[0:64]
    for m in range(1, 4):
        out = jnp.where(which == float(m), blocks[64 * m : 64 * m + 64], out)
    return out


VMEM = pl.BlockSpec(memory_space=pltpu.VMEM)
SMEM = pl.BlockSpec(memory_space=pltpu.SMEM)


def struct(*shape):
    return jax.ShapeDtypeStruct(shape, F32)


def lanes():
    return lax.broadcasted_iota(jnp.int32, (8, 128), 1)


def rows():
    return lax.broadcasted_iota(jnp.int32, (8, 128), 0)


def pack_faces(read_rotor, read_stator, sa, sah, sb, sbh):
    lane = lanes()

    def body(n, carry):
        for read, full, half in ((read_rotor, sa, sah), (read_stator, sb, sbh)):
            one, two = read(n), read(n + 32)
            full[n] = one
            full[n + 32] = two
            half[0, n] = jnp.where(lane < 64, one, pltpu.roll(two, 64, 1))
            half[1, n] = jnp.where(lane < 64, pltpu.roll(one, 64, 1), two)
        return carry

    lax.fori_loop(0, 32, body, 0)


def pack_halos(read, hs, cs):
    lane = lanes()
    zero = jnp.zeros((8, 128), F32)

    def body(n, carry):
        upper, lower = carry
        side, i = n // 8, lax.rem(n, 8)
        for k in range(8):
            hs[0, n, pl.ds(k, 1), :] = read(64 * i + 56 + k, side)[7:8, :]
            hs[1, n, pl.ds(k, 1), :] = read(64 * i + k, side)[0:1, :]
        for j in range(8):
            place = 8 * n + j
            last = pltpu.roll(read(64 * i + 8 * j + 7, side), lax.rem(place + 1, 128), 1)
            first = pltpu.roll(read(64 * i + 8 * j, side), place, 1)
            upper = jnp.where(lane == place, last, upper)
            lower = jnp.where(lane == place, first, lower)
        return upper, lower

    upper, lower = lax.fori_loop(0, 16, body, (zero, zero))
    cs[0] = upper
    cs[1] = lower


def turn(main, near, by):
    lane = lanes()
    first = jnp.where(by > 0, 128 - by, 0)
    end = jnp.where(by > 0, 128, -by)
    missing = jnp.logical_and(lane >= first, lane < end)
    picked = jnp.where(missing, near, main)
    return pltpu.roll(picked, lax.rem(by + 128, 128), 1)


PACKED = [
    struct(64, 8, 128),
    struct(2, 32, 8, 128),
    struct(65, 8, 128),
    struct(2, 33, 8, 128),
    struct(2, 16, 8, 128),
    struct(2, 8, 128),
]


def opening(rhs, face_map, interp, sa, sah, sb, sbh, hs, cs, weights):
    pack_faces(lambda n: rhs[n + 448, 0], lambda n: rhs[n, 1], sa, sah, sb, sbh)
    which = face_map[...].astype(F32)
    sb[64] = which
    sbh[0, 32] = which
    sbh[1, 32] = which
    pack_halos(lambda n, side: rhs[n, side], hs, cs)
    blocks = interp[...]
    weights[0] = split_columns(blocks.reshape(256, 64))
    turned = jnp.concatenate(
        [
            jnp.concatenate([blocks[0], blocks[1]], axis=1).T,
            jnp.concatenate([blocks[2], blocks[3]], axis=1).T,
        ],
        axis=0,
    )
    weights[1] = split_columns(turned)


def opened(right_side, face_map, interp):
    return pl.pallas_call(
        opening,
        out_shape=PACKED + [jax.ShapeDtypeStruct((2, 256, 256), BF16)],
        in_specs=[VMEM] * 3,
        out_specs=[VMEM] * 7,
        compiler_params=pltpu.CompilerParams(vmem_limit_bytes=32 * 1024 * 1024),
    )(right_side, face_map, interp)


def exchange(nb, nr, hop, *refs):
    sa, sah, sb, sbh, hs, cs, ra, rah, rb, rbh, hrecv, crecv, send_sem, recv_sem = refs
    blk = lax.axis_index("blk")
    rad = lax.axis_index("rad")

    def along(by):
        return {"blk": lax.rem(blk + by + 2 * nb, nb), "rad": rad}

    def across(by):
        return {"blk": blk, "rad": lax.rem(rad + by + nr, nr)}

    plan = []
    for src, half, dst, dhalf, way in ((sa, sah, ra, rah, 1), (sb, sbh, rb, rbh, -1)):
        for source, target, by in (
            (src, dst, way * hop),
            (half.at[0], dhalf.at[0], way * hop - 1),
            (half.at[1], dhalf.at[1], way * hop + 1),
        ):
            plan.append((source, target, along(by) if by % nb else None))
    plan += [
        (hs.at[0], hrecv.at[0], across(1)),
        (hs.at[1], hrecv.at[1], across(-1)),
        (cs.at[0], crecv.at[0], along(1)),
        (cs.at[1], crecv.at[1], along(-1)),
    ]
    peers = [peer for _, _, peer in plan if peer is not None]
    barrier = pltpu.get_barrier_semaphore()
    for peer in peers:
        pl.semaphore_signal(barrier, inc=1, device_id=peer, device_id_type=MESH)
    pl.semaphore_wait(barrier, len(peers))
    copies = []
    for n, (source, target, peer) in enumerate(plan):
        if peer is None:
            copy = pltpu.make_async_copy(source, target, recv_sem.at[n])
        else:
            copy = pltpu.make_async_remote_copy(
                source,
                target,
                send_sem.at[n],
                recv_sem.at[n],
                device_id=peer,
                device_id_type=MESH,
            )
        copy.start()
        copies.append(copy)
    for copy in copies:
        copy.wait()


def exchanged(nb, nr, hop, *packed):
    return pl.pallas_call(
        functools.partial(exchange, nb, nr, hop),
        out_shape=PACKED,
        in_specs=[VMEM] * 6,
        out_specs=[VMEM] * 6,
        scratch_shapes=[pltpu.SemaphoreType.DMA((10,)), pltpu.SemaphoreType.DMA((10,))],
        compiler_params=pltpu.CompilerParams(collective_id=hop, has_side_effects=True),
    )(*packed)


def reduce_kernel(nb, nr, part, scal, source, one, two, send_sem, recv_sem):
    blk = lax.axis_index("blk")
    rad = lax.axis_index("rad")

    def plane_peer(d):
        return {"blk": (blk // 16) * 16 + lax.rem(lax.rem(blk, 16) + d, 16), "rad": rad}

    def line_peer(d):
        place = lax.rem((blk // 16) * nr + rad + d, 2 * nr)
        return {"blk": (place // nr) * 16 + lax.rem(blk, 16), "rad": lax.rem(place, nr)}

    stages = (
        (16, lax.rem(blk, 16), plane_peer, one),
        (2 * nr, (blk // 16) * nr + rad, line_peer, two),
    )
    barrier = pltpu.get_barrier_semaphore()
    for count, _, peer, _ in stages:
        for d in range(1, count):
            pl.semaphore_signal(barrier, inc=1, device_id=peer(d), device_id_type=MESH)
    pl.semaphore_wait(barrier, 14 + 2 * nr)
    tile = part[...]
    for stage, (count, place, peer, buf) in enumerate(stages):
        source[stage] = tile
        buf[place] = tile
        for d in range(1, count):
            pltpu.make_async_remote_copy(
                source.at[stage],
                buf.at[place],
                send_sem.at[stage],
                recv_sem.at[stage],
                device_id=peer(d),
                device_id_type=MESH,
            ).start()
        whole = buf.at[pl.ds(0, count - 1)]
        pltpu.make_async_copy(whole, whole, recv_sem.at[stage]).wait()
        tile = buf[0]
        for n in range(1, count):
            tile = tile + buf[n]
        pltpu.make_async_copy(whole, whole, send_sem.at[stage]).wait()
    totals = jnp.sum(tile, axis=1, keepdims=True)
    pq, rq, qq, rr = [jnp.broadcast_to(totals[n : n + 1], (8, 128)) for n in range(4)]
    alpha = rr / pq
    fresh = rr - 2.0 * alpha * rq + alpha * alpha * qq
    scal[0] = alpha
    scal[1] = fresh / rr


def reduced(nb, nr, part):
    return pl.pallas_call(
        functools.partial(reduce_kernel, nb, nr),
        out_shape=struct(2, 8, 128),
        in_specs=[VMEM],
        out_specs=VMEM,
        scratch_shapes=[
            pltpu.VMEM((2, 8, 128), F32),
            pltpu.VMEM((16, 8, 128), F32),
            pltpu.VMEM((2 * nr, 8, 128), F32),
            pltpu.SemaphoreType.DMA((2,)),
            pltpu.SemaphoreType.DMA((2,)),
        ],
        compiler_params=pltpu.CompilerParams(collective_id=nb, has_side_effects=True),
    )(part)


def step(first, last, nr, *refs):
    refs = list(refs)
    take = lambda n: [refs.pop(0) for _ in range(n)]
    offset, rold, cf, geom, weights = take(5)
    ra, rah, rb, rbh, hrecv, crecv = take(6)
    if first:
        (face_map,) = take(1)
        alpha = beta = None
    else:
        scal, pold, qold, maps = take(4)
        olds = take(8)
        alpha, beta = scal[0], scal[1]
    p, q, part = take(3)
    if not first:
        (r,) = take(1)
    else:
        r = rold
        (maps,) = take(1)
    news = take(8)
    if not last:
        packed = take(6)
    rad = lax.axis_index("rad")
    lane, row = lanes(), rows()
    zero = jnp.zeros((8, 128), F32)
    shift = lax.rem(offset[0] + 64, 128) - 64
    if first:
        maps[0] = face_map[...].astype(F32)
        maps[1] = turn(rb[64], jnp.where(lane < 64, rbh[0, 32], rbh[1, 32]), -shift)
    a_res, a_dir, b_res, b_dir, h_res, h_dir, c_res, c_dir = news

    def refresh(slot, place, fresh):
        res, ahead = news[slot], news[slot + 1]
        if first:
            res[place] = fresh
            ahead[place] = fresh
        else:
            value = olds[slot][place] - alpha * fresh
            res[place] = value
            ahead[place] = value + beta * olds[slot + 1][place]

    def columns(t, total):
        for s in range(2):
            v = []
            for i in range(8):
                n = 64 * i + t
                if first:
                    value = rold[n, s]
                    ahead = value
                else:
                    value = rold[n, s] - alpha * qold[n, s]
                    r[n, s] = value
                    ahead = value + beta * pold[n, s]
                total = total + value * value
                p[n, s] = ahead
                v.append(ahead)
            g = geom[0, s]
            for i, value in enumerate(line_apply(v)):
                q[64 * i + t, s] = cf[64 * i + t, s] * v[i] + g * value
        return total

    rr = lax.fori_loop(0, 64, columns, zero)

    def halo_step(n, carry):
        for side in range(2):
            refresh(4, (side, n), hrecv[side, n])
        return carry

    lax.fori_loop(0, 16, halo_step, 0)
    for side in range(2):
        refresh(6, side, crecv[side])

    def face_step(n, carry):
        for main, half, slot, by in ((ra, rah, 0, shift), (rb, rbh, 2, -shift)):
            low, high = half[0, n], half[1, n]
            mixed = pltpu.roll(jnp.where(lane < 64, high, low), 64, 1)
            nears = (jnp.where(lane < 64, low, mixed), jnp.where(lane < 64, mixed, high))
            for place, near in zip((n, n + 32), nears):
                refresh(slot, place, turn(main[place], near, by))
        return carry

    lax.fori_loop(0, 32, face_step, 0)

    def pair(half, carry):
        jumps = []
        here = []
        for u in range(2):
            rr_ = 2 * half + u
            own = p[pl.ds(448, 64), 0, rr_, :]
            over = a_dir[:, rr_, :]
            mapped = jnp.dot(
                weights[0],
                split_rows(jnp.concatenate([own, over], axis=1)),
                preferred_element_type=F32,
            )
            mine = maps[1, pl.ds(rr_, 1), :]
            theirs = maps[0, pl.ds(rr_, 1), :]
            jumps.append(choose(mapped[:, :128], mine) - b_dir[:, rr_, :])
            here.append(mine)
            jump = choose(mapped[:, 128:], theirs) - p[pl.ds(0, 64), 1, rr_, :]
            q[pl.ds(0, 64), 1, rr_, :] = q[pl.ds(0, 64), 1, rr_, :] - jump
        back = jnp.dot(
            weights[1],
            split_rows(jnp.concatenate(jumps, axis=1)),
            preferred_element_type=F32,
        )
        for u in range(2):
            rr_ = 2 * half + u
            added = choose(back[:, 128 * u : 128 * u + 128], here[u])
            q[pl.ds(448, 64), 0, rr_, :] = q[pl.ds(448, 64), 0, rr_, :] + added
        return carry

    lax.fori_loop(0, 4, pair, 0)

    upper_open = row < jnp.where(rad < nr - 1, 8, 7)
    lower_open = row >= jnp.where(rad > 0, 0, 1)

    def plane(t, sums):
        s, i = t // 8, lax.rem(t, 8)
        base = 64 * i
        g_r, g_c = geom[1, s], geom[2, s]
        after, before = c_dir[1], c_dir[0]
        for j in range(8):
            v = [p[base + 8 * j + k, s] for k in range(8)]
            w = line_apply(v)
            place = 64 * s + 8 * i + j
            nxt = jnp.where(
                lane == 127, pltpu.roll(after, 127 - place, 1), pltpu.roll(v[0], 127, 1)
            )
            prv = jnp.where(
                lane == 0,
                pltpu.roll(before, lax.rem(128 - place, 128), 1),
                pltpu.roll(v[7], 1, 1),
            )
            for k in range(8):
                value = q[base + 8 * j + k, s] + g_c * w[k]
                if k == 7:
                    value = value + (v[7] - nxt)
                if k == 0:
                    value = value - (prv - v[0])
                q[base + 8 * j + k, s] = value
        pq, rq, qq = zero, zero, zero
        for k in range(8):
            v = [p[base + 8 * j + k, s] for j in range(8)]
            w = line_apply(v)
            above = h_dir[1, 8 * s + i, pl.ds(k, 1), :]
            below = h_dir[0, 8 * s + i, pl.ds(k, 1), :]
            nxt = jnp.where(row == 7, above, pltpu.roll(v[0], 7, 0))
            prv = jnp.where(row == 0, below, pltpu.roll(v[7], 1, 0))
            for j in range(8):
                n = base + 8 * j + k
                value = q[n, s] + g_r * w[j]
                if j == 7:
                    value = value + jnp.where(upper_open, v[7] - nxt, 0.0)
                if j == 0:
                    value = value - jnp.where(lower_open, prv - v[0], 0.0)
                q[n, s] = value
                pq = pq + v[j] * value
                rq = rq + r[n, s] * value
                qq = qq + value * value
        return sums[0] + pq, sums[1] + rq, sums[2] + qq

    pq, rq, qq = lax.fori_loop(0, 16, plane, (zero, zero, zero))
    tile = zero
    for n, one in enumerate((pq, rq, qq, rr)):
        tile = jnp.where(row == n, jnp.sum(one, axis=0, keepdims=True), tile)
    part[...] = tile
    if not last:
        sa, sah, sb, sbh, hs, cs = packed
        pack_faces(lambda n: q[n + 448, 0], lambda n: q[n, 1], sa, sah, sb, sbh)
        for ref in (sb.at[64], sbh.at[0, 32], sbh.at[1, 32]):
            ref[...] = zero
        pack_halos(lambda n, side: q[n, side], hs, cs)


FACES = [struct(64, 8, 128)] * 4 + [struct(2, 16, 8, 128)] * 2 + [struct(2, 8, 128)] * 2


def stepped(first, last, nr, offset, rold, cf, geom, weights, received, *rest):
    field = struct(*rold.shape)
    outs = [field, field, struct(8, 128)]
    outs += [struct(2, 8, 128)] if first else [field]
    outs += FACES
    if not last:
        outs += PACKED
    args = [offset, rold, cf, geom, weights, *received, *rest]
    aliases = {}
    if not first:
        aliases = {12: 0, 13: 1}
        aliases.update({15 + n: 4 + n for n in range(8)})
    return pl.pallas_call(
        functools.partial(step, first, last, nr),
        out_shape=outs,
        in_specs=[SMEM] + [VMEM] * (len(args) - 1),
        out_specs=[VMEM] * len(outs),
        input_output_aliases=aliases,
        compiler_params=pltpu.CompilerParams(vmem_limit_bytes=LIMIT * 1024 * 1024),
    )(*args)


LIMIT = 48

def finish(r0, r1, r2, q, c, x_out, r_out):
    c0, c1, c2 = c[0][None, None], c[1][None, None], c[2][None, None]
    last = r2[...]
    x_out[...] = c0 * r0[...] + c1 * r1[...] + c2 * last
    r_out[...] = last - c2 * q[...]


def finished(r0, r1, r2, q, c):
    points = 32
    block = pl.BlockSpec((points,) + r0.shape[1:], lambda n: (n, 0, 0, 0))
    return pl.pallas_call(
        finish,
        grid=(r0.shape[0] // points,),
        out_shape=[jax.ShapeDtypeStruct(r0.shape, F32)] * 2,
        in_specs=[block] * 4 + [pl.BlockSpec(c.shape, lambda n: (0, 0, 0))],
        out_specs=[block] * 2,
        compiler_params=pltpu.CompilerParams(vmem_limit_bytes=32 * 1024 * 1024),
    )(r0, r1, r2, q, c)


HOPS = None


def on_device(nb, nr, right_side, coefficient, geometry, interp, face_map, offset):
    cells = nb * right_side.shape[3]
    rotation = lax.rem(offset[0], cells)
    hops = lax.rem((rotation + 64) // 128, nb)

    def swap(packed):
        if HOPS is None:
            branches = [functools.partial(exchanged, nb, nr, hop) for hop in range(nb)]
            return lax.switch(hops, branches, *packed)
        return exchanged(nb, nr, HOPS, *packed)

    *packed, weights = opened(right_side, face_map, interp)
    got = swap(packed)
    p, q, part, maps, *rest = stepped(
        True, False, nr, offset, right_side, coefficient, geometry, weights, got, face_map
    )
    states, packed = rest[:8], rest[8:]
    residuals = [right_side]
    factors = []
    for it in range(1, ITERS):
        factors.append(reduced(nb, nr, part))
        got = swap(packed)
        p, q, part, r, *rest = stepped(
            False,
            it == ITERS - 1,
            nr,
            offset,
            residuals[-1],
            coefficient,
            geometry,
            weights,
            got,
            factors[-1],
            p,
            q,
            maps,
            *states,
        )
        states, packed = rest[:8], rest[8:]
        residuals.append(r)
    factors.append(reduced(nb, nr, part))
    (a0, b0), (a1, b1), (a2, _) = factors
    one = a1 + b1 * a2
    weighed = jnp.stack([a0 + b0 * one, one, a2])
    return tuple(finished(*residuals, q, weighed))


def solution(mesh):
    nb, nr = mesh.shape["blk"], mesh.shape["rad"]
    field = P(None, None, "rad", "blk")
    return jax.shard_map(
        functools.partial(on_device, nb, nr),
        mesh=mesh,
        in_specs=(field, field, field, P(), P("rad", "blk"), P()),
        out_specs=(field, field),
        check_vma=False,
    )
```

time: 970 us -> 271 us (0.28); the launches traced: 958 us -> 270 us
  blocking collectives: 321 us -> 0 us
  Pallas kernels: 0 us -> 244 us
  local copies, waits for them, and re-layouts: 212 us -> 24 us
  matrix products: 147 us -> 0 us
  other arithmetic: 122 us -> 0.69 us
  starting transfers between devices: 85.1 us -> 0 us
  waiting for transfers between devices: 62 us -> 0 us
    psum x5 -> x0, blocking collectives: 321 us -> none  [the longest x3 193 us: squares_sum(): return lax.psum(jnp.sum(residual * residual), ('blk', 'rad'))]
    pallas_call x0 -> x11, Pallas kernels: none -> 244 us  [the longest x3 101 us: exchanged(): pl.pallas_call(functools.partial(exchange, nb, nr, hop), out_shape=PACKED...]
    dot_general x24 -> x0, matrix products: 147 us -> none  [the longest x3 40.7 us: element_part(): jnp.einsum('ai,ajkx->ijkx', derivative, grad_one * factors[0], precision=...]
    scatter-add x9 -> x0, local copies, waits for them, and re-layouts: 95.4 us -> none  [the longest x3 42.8 us: on_device(): result = result.at[:, :, 0].add(-PENALTY * circ_back)]
    ppermute x48 -> x0, starting transfers between devices: 85.1 us -> none  [the longest x36 47.4 us: from_behind(): lax.ppermute(array, axis, [(i, (i + by) % size) for i in range(size)])]
    ppermute x48 -> x0, waiting for transfers between devices: 62 us -> none  [the longest x36 62 us: from_behind(): lax.ppermute(array, axis, [(i, (i + by) % size) for i in range(size)])]
    add x9 -> x1, other arithmetic: 36.8 us -> 0.68 us  [on_device(): weighed = jnp.stack([a0 + b0 * one, one, a2])]
    another operation x22 -> x0, local copies, waits for them, and re-layouts: 32.1 us -> none  [the longest x3 14.8 us: element_part(): flat_nodes = nodal.reshape(8, 8, 8, -1)]
  transfers between devices with their start and end apart: 48 -> 0, of which waited for: 20 -> 0; matrix products, arithmetic and copies ran while one was open for 38% -> 0% of each run, Pallas kernels for 0% -> 0%
where the time goes in v1:
time: 271 us; the launch traced here: 270 us
  Pallas kernels  244 us (90%)
  local copies, waits for them, and re-layouts  24 us (9%)
    pallas_call x3, Pallas kernels, exchanged(): pl.pallas_call(functools.partial(exchange, nb, nr, hop), out_shape=PACKED...  101 us
    pallas_call x3, Pallas kernels, stepped(): pl.pallas_call(functools.partial(step, first, last, nr), out_shape=outs,...  79.1 us
    pallas_call x3, Pallas kernels, reduced(): pl.pallas_call(functools.partial(reduce_kernel, nb, nr), out_shape=struct...  52.8 us
    unnamed x40, local copies, waits for them, and re-layouts  24 us
    pallas_call x1, Pallas kernels, finished(): pl.pallas_call(finish, grid=(r0.shape[0] // points,), out_shape=[jax.Shap...  6.82 us

profile of v1, /device:TPU:1, one launch (start us, length us, event | category | flops | bytes accessed | tf_op | source)
XLA Modules:
  0.0 270.3 jit_solution(16356298383775501655)
XLA Ops:
  1.3 2.2 copy-done
  3.5 0.9 copy-done.10
  5.1 3.9 %shard_map.77 = (f32[64,8,128]{2,1,0:T(8,128)S(1)}, f32[2,32,8,128]{3,2,1,0:T(8,128)S(1)}, f32[65,8,128]{2,1,0:T(8,128)S(1)}, f32[2,33,8,128]{3,2,1,0:T(8,128)S(...) custom-call(f32[512,2,8,128]{3,2,1,0:T(8,128)S(1)} %copy-done, ...), custom_call_target="tpu_custom_call" | custom-call | tf_op jit(solution)/shard_map/pallas_call | solution.py:162
  9.1 34.3 %conditional.3 = ((f32[64,8,128]{2,1,0:T(8,128)}, f32[2,32,8,128]{3,2,1,0:T(8,128)}, f32[65,8,128]{2,1,0:T(8,128)S(1)}, f32[2,33,8,128]{3,2,1,0:T(8,128)S(1)}, f...) conditional(s32[]{:T(128)} %clamp.2, (f32[64,8,128]{2,1,0:T(8,128)S(1)}, ...), branch_computations={%region_0.1_spmd, %region_1.2_spmd, %region_2.3_spmd, %region_3.4_... | conditional | bytes 8 | solution.py:527
  9.1 34.3 %branch_21_fun.3 = (f32[64,8,128]{2,1,0:T(8,128)}, f32[2,32,8,128]{3,2,1,0:T(8,128)}, f32[65,8,128]{2,1,0:T(8,128)S(1)}, f32[2,33,8,128]{3,2,1,0:T(8,128)S(1)}, ...) custom-call(f32[64,8,128]{2,1,0:T(8,128)S(1)} %get-tuple-element.1278.refs_0_, ...), custom_call_target="tpu_custom_call" | custom-call | tf_op jit(solution)/shard_map/cond/branch_21_fun/pallas_call | solution.py:221
  43.4 23.3 %shard_map.78 = (f32[512,2,8,128]{3,2,1,0:T(8,128)S(1)}, f32[512,2,8,128]{3,2,1,0:T(8,128)}, f32[8,128]{1,0:T(8,128)S(1)}, f32[2,8,128]{2,1,0:T(8,128)S(1)}, f32...) custom-call(s32[1]{0:T(128)} %copy.624.refs_0_, ...), custom_call_target="tpu_custom_call" | custom-call | tf_op jit(solution)/shard_map/pallas_call | solution.py:484
  66.8 2.0 copy-done.4
  69.4 36.1 %conditional.4 = ((f32[64,8,128]{2,1,0:T(8,128)}, f32[2,32,8,128]{3,2,1,0:T(8,128)}, f32[65,8,128]{2,1,0:T(8,128)S(1)}, f32[2,33,8,128]{3,2,1,0:T(8,128)S(1)}, f...) conditional(s32[]{:T(128)} %clamp.2, (f32[64,8,128]{2,1,0:T(8,128)S(1)}, ...), branch_computations={%region_32.33_spmd, %region_33.34_spmd, %region_34.35_spmd, %regio... | conditional | bytes 8 | solution.py:527
  69.4 36.1 %branch_21_fun.4 = (f32[64,8,128]{2,1,0:T(8,128)}, f32[2,32,8,128]{3,2,1,0:T(8,128)}, f32[65,8,128]{2,1,0:T(8,128)S(1)}, f32[2,33,8,128]{3,2,1,0:T(8,128)S(1)}, ...) custom-call(f32[64,8,128]{2,1,0:T(8,128)S(1)} %get-tuple-element.1470.refs_0_, ...), custom_call_target="tpu_custom_call" | custom-call | tf_op jit(solution)/shard_map/cond/branch_21_fun/pallas_call | solution.py:221
  105.5 22.0 %shard_map.79.refs_11_ = f32[2,8,128]{2,1,0:T(8,128)} custom-call(f32[8,128]{1,0:T(8,128)} %copy-done.18), custom_call_target="tpu_custom_call" | custom-call | tf_op jit(solution)/shard_map/pallas_call | solution.py:279
  127.5 2.2 copy-done.5
  130.4 29.8 %shard_map.80 = (f32[512,2,8,128]{3,2,1,0:T(8,128)S(1)}, f32[512,2,8,128]{3,2,1,0:T(8,128)}, f32[8,128]{1,0:T(8,128)S(1)}, f32[512,2,8,128]{3,2,1,0:T(8,128)}, f...) custom-call(s32[1]{0:T(128)} %copy.624.refs_0_, ...), custom_call_target="tpu_custom_call", output_to_operand_aliasing={{0}: (12, {}), {1}: (13, {}), {4}: (15, {}), {5}: (16, {}),... | custom-call | tf_op jit(solution)/shard_map/pallas_call | solution.py:484
  160.1 2.0 copy-done.6
  162.7 31.0 %conditional.5 = ((f32[64,8,128]{2,1,0:T(8,128)}, f32[2,32,8,128]{3,2,1,0:T(8,128)}, f32[65,8,128]{2,1,0:T(8,128)S(1)}, f32[2,33,8,128]{3,2,1,0:T(8,128)S(1)}, f...) conditional(s32[]{:T(128)} %clamp.2, (f32[64,8,128]{2,1,0:T(8,128)S(1)}, ...), branch_computations={%region_64.65_spmd, %region_65.66_spmd, %region_66.67_spmd, %regio... | conditional | bytes 8 | solution.py:527
  162.7 31.0 %branch_21_fun.5 = (f32[64,8,128]{2,1,0:T(8,128)}, f32[2,32,8,128]{3,2,1,0:T(8,128)}, f32[65,8,128]{2,1,0:T(8,128)S(1)}, f32[2,33,8,128]{3,2,1,0:T(8,128)S(1)}, ...) custom-call(f32[64,8,128]{2,1,0:T(8,128)S(1)} %get-tuple-element.1662.refs_0_, ...), custom_call_target="tpu_custom_call" | custom-call | tf_op jit(solution)/shard_map/cond/branch_21_fun/pallas_call | solution.py:221
  193.7 18.1 %shard_map.81.refs_11_ = f32[2,8,128]{2,1,0:T(8,128)} custom-call(f32[8,128]{1,0:T(8,128)} %copy-done.17), custom_call_target="tpu_custom_call" | custom-call | tf_op jit(solution)/shard_map/pallas_call | solution.py:279
  211.8 2.2 copy-done.7
  214.7 26.0 %shard_map.82 = (f32[512,2,8,128]{3,2,1,0:T(8,128)S(1)}, f32[512,2,8,128]{3,2,1,0:T(8,128)}, f32[8,128]{1,0:T(8,128)S(1)}, f32[512,2,8,128]{3,2,1,0:T(8,128)}, f...) custom-call(s32[1]{0:T(128)} %copy.624.refs_0_, ...), custom_call_target="tpu_custom_call", output_to_operand_aliasing={{0}: (12, {}), {1}: (13, {}), {4}: (15, {}), {5}: (16, {}),... | custom-call | tf_op jit(solution)/shard_map/pallas_call | solution.py:484
  241.3 12.8 %shard_map.83 = f32[2,8,128]{2,1,0:T(8,128)} custom-call(f32[8,128]{1,0:T(8,128)} %copy-done.19), custom_call_target="tpu_custom_call" | custom-call | tf_op jit(solution)/shard_map/pallas_call | solution.py:279
  254.8 2.2 copy-done.1
  256.9 2.2 copy-done.2
  259.1 2.2 copy-done.3
  261.3 2.2 copy-done.8
  263.5 6.8 %shard_map.84 = (f32[512,2,8,128]{3,2,1,0:T(8,128)}, f32[512,2,8,128]{3,2,1,0:T(8,128)}) custom-call(f32[512,2,8,128]{3,2,1,0:T(8,128)S(1)} %copy-done.1, f32[512,2,8,128]{3,2,1,0:T(8,128)S(1)} %copy-done.3, f32[512,2,8,128]{3,2,1,0:T(8,128)S(1)} %copy-done.8, f32[512,2,8,128]{3,2,1,0:T(8,128)S(1)} %copy-done.2, f32[3,8,128]{2,1,0:T(8,128)S(1)} %pad_maximum_fusion.c), custom_call_target="tpu_custom_call" | custom-call | tf_op jit(solution)/shard_map/pallas_call | solution.py:506
  (32 shorter events, 4.6 us)
Async XLA Ops:
  1.3 2.2 copy-start
  3.5 0.9 copy-start.10
  4.4 0.7 copy-start.15
  9.0 34.4 %copy-start.9 = (f32[3,2,8,128]{3,2,1,0:T(8,128)S(1)}, f32[3,2,8,128]{3,2,1,0:T(8,128)}, u32[]{:S(2)}) copy-start(f32[3,2,8,128]{3,2,1,0:T(8,128)} %refs_3_.5) | copy-start | bytes 73732
  9.1 34.4 %copy-start.16 = (s32[8,128]{1,0:T(8,128)S(1)}, s32[8,128]{1,0:T(8,128)}, u32[]{:S(2)}) copy-start(s32[8,128]{1,0:T(8,128)} %refs_11_.1) | copy-start | bytes 12292
  66.8 2.0 copy-start.4
  68.8 0.6 copy-start.18
  127.5 2.2 copy-start.5
  129.7 0.7 copy-start.11
  160.1 2.0 copy-start.6
  162.1 0.6 copy-start.17
  211.8 2.2 copy-start.7
  214.0 0.7 copy-start.13
  214.7 39.4 %copy-start.12 = (f32[2,8,128]{2,1,0:T(8,128)S(1)}, f32[2,8,128]{2,1,0:T(8,128)}, u32[]{:S(2)}) copy-start(f32[2,8,128]{2,1,0:T(8,128)} %shard_map.79.refs_11_) | copy-start | bytes 24580
  214.7 39.4 %copy-start.14 = (f32[2,8,128]{2,1,0:T(8,128)S(1)}, f32[2,8,128]{2,1,0:T(8,128)}, u32[]{:S(2)}) copy-start(f32[2,8,128]{2,1,0:T(8,128)} %shard_map.81.refs_11_) | copy-start | bytes 24580
  240.7 0.6 copy-start.19
  254.8 2.2 copy-start.1
  256.9 2.2 copy-start.2
  259.1 2.2 copy-start.3
  261.3 2.2 copy-start.8
